TPU v7x, 32 devices: a whole 2x2x4 slice. The times are simulated.
32 devices in a mesh: grp: 2 (over core), lat: 16 (over z, y, x).
Axes of the slice: x: 2, y: 2, z: 4, core: 2. Of those that a mesh axis runs over, the one named last changes fastest.
Arguments:
- spectral_state: bfloat16 [2, 640, 64, 640], P('grp', 'lat'), may hold values from -6 to 6
- cotangent: bfloat16 [2, 640, 64, 640], P('grp', 'lat'), may hold values from -6 to 6
- legendre: bfloat16 [640, 640, 128], P('lat'), as said below
- quadrature: float32 [128], replicated, may hold values from 0.2 to 1
- damping: float32 [32], replicated, may hold values from 0.05 to 20
- physics_in: bfloat16 [512, 32], replicated, may hold values from -1 to 1
- physics_bias: float32 [512], replicated, may hold values from -3 to 3
- physics_out: bfloat16 [32, 512], replicated, may hold values from -0.25 to 0.25
Outputs:
- grad_state: float32 [2, 640, 64, 640], P('grp', 'lat')
- grad_in: float32 [512, 32], replicated
- grad_bias: float32 [512], replicated
- grad_out: float32 [32, 512], replicated
Inputs may be any that keep to these rules, and one draw needn't show every extreme that they name: legendre[m, l, p] is zero for every degree l below the wavenumber m, and generally nonzero otherwise.
All inputs are finite; a program needn't handle non-finite values.
Results may differ from a plain program's by a relative error of at most 0.015.
Values may be sent and summed in bfloat16 or wider, within the bound.
No kernel may reach another device: no remote copies, remote signals or barrier semaphores. Data moves between devices by JAX's collectives and lax.ppermute only.
A program may use at most 192 MiB of HBM per device.

v0:
```python
import functools
import math

import jax
import jax.numpy as jnp
import numpy as np
import ml_dtypes
from jax import lax
from jax.experimental import pallas as pl
from jax.experimental.pallas import tpu as pltpu
from jax.sharding import PartitionSpec as P

NLON = 2560
MIB = 1024 * 1024
F32 = jnp.float32
BF16 = jnp.bfloat16
PARTS = 2
SLOTS = 256
UNIT = 128
HBM = pl.BlockSpec(memory_space=pl.ANY)


def longitude_table(waves, points):
    slots = points // 2
    phase = np.arange(waves)[:, None] * np.arange(slots)[None, :] % points
    angle = phase * (2.0 * math.pi / points)
    scale = math.sqrt(2.0 / points)
    both = np.concatenate([np.cos(angle) * scale, -np.sin(angle) * scale])
    return both.astype(np.float32).astype(ml_dtypes.bfloat16)


def dot(a, b):
    return jnp.dot(a, b, preferred_element_type=F32)


def dot_nt(a, b):
    return lax.dot_general(a, b, (((1,), (1,)), ((), ())), preferred_element_type=F32)


def params(mib):
    return pltpu.CompilerParams(vmem_limit_bytes=mib * MIB, dimension_semantics=("arbitrary",))


def whole(*shape):
    return pl.BlockSpec(shape, lambda i: (0,) * len(shape))


def block_of(waves, most):
    return max(size for size in range(1, most + 1) if waves % size == 0)


def set_factor(factor, damping):
    width, degrees = factor.shape
    chans = width // 2
    lanes = 128
    spread = jnp.broadcast_to(damping[...], (lanes, chans)).T
    for start in range(0, degrees, lanes):
        degree = (lax.broadcasted_iota(jnp.int32, (chans, lanes), 1) + start).astype(F32)
        ratio = degree * (degree + 1.0) / (degrees * (degrees + 1.0))
        piece = 1.0 / (1.0 + spread * ratio)
        factor[:chans, start : start + lanes] = piece
        factor[chans:, start : start + lanes] = piece


def copies_of(pairs, sems):
    copies = [pltpu.make_async_copy(src, dst, sems.at[k]) for k, (src, dst) in enumerate(pairs)]
    for copy in copies:
        copy.start()
    return copies


def forward_kernel(ranks, block, part, *refs):
    spec_h, cot_h, leg_h, damping, quad, out = refs[:6]
    spec, cot, leg, rows, factor, sems = refs[6:]
    own, width, _ = spec.shape
    chans = width // 2
    lat = leg.shape[2]
    near = lat // ranks // 2 // PARTS
    span = ranks * near

    def moves(c):
        here = pl.ds(c * block, block)
        return [
            pltpu.make_async_copy(src.at[here], dst.at[here], sems.at[c, k])
            for k, (src, dst) in enumerate(((spec_h, spec), (cot_h, cot), (leg_h, leg)))
        ]

    ahead = 4
    for c in range(min(ahead, own // block)):
        for move in moves(c):
            move.start()
    set_factor(factor, damping)

    def step(c, carry):
        for move in moves(c):
            move.wait()

        @pl.when(c + ahead < own // block)
        def _():
            for move in moves(c + ahead):
                move.start()

        weight = quad[...]
        for k in range(block):
            i = c * block + k
            tend = (cot[i].astype(F32) * factor[...]).astype(BF16)
            state = spec[i]
            stacked = jnp.concatenate(
                [state[:chans], tend[:chans], state[chans:], tend[chans:]], axis=0
            )
            res = dot(stacked, leg[i])
            res = jnp.concatenate(
                [
                    res[:chans],
                    res[chans : 2 * chans] * weight,
                    res[2 * chans : 3 * chans],
                    res[3 * chans :] * weight,
                ],
                axis=0,
            )
            res = res.astype(BF16).T.astype(F32)
            for side in range(2):
                start = (side * PARTS + part) * span
                rows[pl.ds(side * span * own + i, span, stride=own), :] = res[start : start + span]
        return carry

    lax.fori_loop(0, own // block, step, 0)
    size = near * own
    for d in range(ranks):
        for side in range(2):
            start = (side * ranks + d) * size
            out[d, side * size : (side + 1) * size, :] = rows[start : start + size, :].astype(BF16)


def forward(spectral, cot, legendre, damping, quad, ranks, part):
    own, width, degrees = spectral.shape
    lat = legendre.shape[2]
    block = block_of(own, 4)
    shape = (ranks, lat // ranks // PARTS * own, 2 * width)
    return pl.pallas_call(
        functools.partial(forward_kernel, ranks, block, part),
        grid=(1,),
        in_specs=[HBM] * 3 + [whole(*damping.shape), whole(1, lat)],
        out_specs=whole(*shape),
        out_shape=jax.ShapeDtypeStruct(shape, BF16),
        scratch_shapes=[
            pltpu.VMEM(spectral.shape, BF16),
            pltpu.VMEM(cot.shape, BF16),
            pltpu.VMEM(legendre.shape, BF16),
            pltpu.VMEM((lat // PARTS * own, 2 * width), F32),
            pltpu.VMEM((width, degrees), F32),
            pltpu.SemaphoreType.DMA((own // block, 3)),
        ],
        compiler_params=params(60),
        name="legendre_forward",
    )(spectral, cot, legendre, damping, quad)


def weights_kernel(w_in, bias, w_out, weights):
    chans, hid = w_in.shape
    width = 2 * chans
    half_bias = bias[...] * 0.5
    high = half_bias.astype(BF16).astype(F32)
    left = half_bias - high
    mid = left.astype(BF16).astype(F32)
    low = left - mid
    stack = jnp.concatenate(
        [
            w_in[...].astype(F32) * 0.5,
            w_out[...].astype(F32) * 0.5,
            high,
            mid,
            low,
            jnp.zeros((13, hid), F32),
        ],
        axis=0,
    ).T.astype(BF16)
    lane = lax.broadcasted_iota(jnp.int32, stack.shape, 1)
    is_out = (lane >= chans) & (lane < width)
    nothing = jnp.zeros_like(stack)
    inward = jnp.where(is_out, nothing, stack)
    outward = jnp.where(is_out, stack, nothing)
    for k in range(0, hid, UNIT):
        weights[2 * k : 2 * k + UNIT, :] = inward[k : k + UNIT]
        weights[2 * k + UNIT : 2 * k + 2 * UNIT, :] = outward[k : k + UNIT]


def column_weights(w_in, bias, w_out):
    chans, hid = w_in.shape
    shape = (2 * hid, 2 * chans + 16)
    return pl.pallas_call(
        weights_kernel,
        grid=(1,),
        in_specs=[whole(*w_in.shape), whole(*bias.shape), whole(*w_out.shape)],
        out_specs=whole(*shape),
        out_shape=jax.ShapeDtypeStruct(shape, BF16),
        compiler_params=params(60),
        name="column_weights",
    )(w_in, bias, w_out)


def column_kernel(ranks, own, first, last, *refs):
    given = 4 if first else 5
    sources, out = refs[:given], refs[given]
    refs = refs[given + 1 :]
    after, refs = refs[0], refs[1:]
    arrived, table, w_in, weights, sums = refs[:5]
    fourier, cols, acts, evens, odds, edge, sems = refs[5:]
    chans, hid = w_in.shape
    waves = ranks * own
    lat_rows = arrived.shape[1] // own
    near = lat_rows // 2
    slots = table.shape[1]
    points = 2 * slots
    scale = math.sqrt(2.0 / points)
    width = 2 * chans
    arrived_h, table_h, w_in_h, weights_h = sources[:4]
    pairs = [(arrived_h, arrived), (w_in_h, w_in), (weights_h, weights)]
    if not first:
        pairs.append((sources[4], sums))
    small = copies_of(pairs, sems)
    moves = []
    for c in range(slots // SLOTS):
        here = pl.ds(c * SLOTS, SLOTS)
        moves.append(
            pltpu.make_async_copy(table_h.at[:, here], table.at[:, here], sems.at[4 + c])
        )
    moves[0].start()
    for p in range(lat_rows):
        cols[p, width:, :] = jnp.ones((16, points), BF16)
    for copy in small:
        copy.wait()
    for move in moves[1:]:
        move.start()
    if first:
        sums[...] = jnp.zeros_like(sums)
    for p in range(lat_rows):
        piece = jnp.concatenate(
            [arrived[s, p * own : (p + 1) * own, :] for s in range(ranks)], axis=0
        ).T
        row = width * p
        fourier[row : row + width, :waves] = piece[:width]
        fourier[row : row + width, waves:] = piece[width:]
    wave = lax.broadcasted_iota(jnp.int32, (waves, 128), 0)
    lane = lax.broadcasted_iota(jnp.int32, (waves, 128), 1)
    alternate = jnp.where(lane == 0, jnp.where(wave % 2 == 0, scale, -scale), 0.0).astype(BF16)
    for c, move in enumerate(moves):
        move.wait()
        here = slice(c * SLOTS, (c + 1) * SLOTS)
        even = dot(fourier[:, :waves], table[:waves, here])
        odd = dot(fourier[:, waves:], table[waves:, here])
        front = (even + odd).astype(BF16)
        rear = even - odd
        if c == 0:
            middle = dot(fourier[:, :waves], alternate)
            lane = lax.broadcasted_iota(jnp.int32, middle.shape, 1)
            rear = jnp.concatenate(
                [jnp.where(lane == 0, middle, rear[:, :128]), rear[:, 128:]], axis=1
            )
        rear = rear.astype(BF16)
        there = slice(slots + c * SLOTS, slots + (c + 1) * SLOTS)
        for p in range(lat_rows):
            cols[p, :width, here] = front[width * p : width * (p + 1)]
            cols[p, :width, there] = rear[width * p : width * (p + 1)]

    together = acts.shape[0]
    span = 512

    def rows_step(g, carry):
        for r in range(together):
            p = g * together + r
            for n in range(0, points, span):
                here = slice(n, n + span)
                columns_here = cols[p, :, here]
                for k in range(0, hid, UNIT):
                    both = dot(weights[2 * k : 2 * k + 2 * UNIT, :], columns_here).astype(BF16)
                    arg = both[:UNIT]
                    th = jnp.tanh(arg)
                    rise = 1 + th
                    act = arg * rise
                    acts[r, k : k + UNIT, here] = act
                    acts[r, hid + k : hid + k + UNIT, here] = both[UNIT:] * (
                        rise + act * (1 - th)
                    )
            grad = dot(w_in[...], acts[r, hid:, :])
            front, rear = grad[:, :slots], grad[:, slots:]
            edge[p] = rear[:, :128].astype(BF16)
            slot = lax.broadcasted_iota(jnp.int32, rear.shape, 1)
            evens[p] = (front + jnp.where(slot == 0, 0.0, rear)).astype(BF16)
            odds[p] = (front - rear).astype(BF16)
            sums[...] += dot_nt(acts[r], cols[p])
        return carry

    lax.fori_loop(0, lat_rows // together, rows_step, 0)

    def joined(ref):
        return ref[...].reshape(chans * lat_rows, ref.shape[2])

    real = dot_nt(table[:waves, :], joined(evens)) + dot_nt(alternate, joined(edge))
    real = real.astype(BF16)
    imag = dot_nt(table[waves:, :], joined(odds)).astype(BF16)
    span = near * chans
    for q in range(near):
        a, b = q * chans, (q + 1) * chans
        piece = jnp.concatenate(
            [real[:, a:b], imag[:, a:b], real[:, span + a : span + b], imag[:, span + a : span + b]],
            axis=1,
        )
        for d in range(ranks):
            out[d, q * own : (q + 1) * own, :] = piece[d * own : (d + 1) * own]
    if not last:
        after[...] = sums[...]
        return
    base = near * own
    turned = sums[...].T
    main = jnp.concatenate([turned[:chans, hid:], turned[chans:width, :hid]], axis=0)
    lanes = 4 * chans
    cuts = range(0, hid, lanes)
    after[...] = turned[width : width + 1, hid:]
    share = width // ranks
    for d in range(ranks):
        rows = [main[d * share : (d + 1) * share, c : c + lanes] for c in cuts]
        rows = jnp.concatenate(rows, axis=0).astype(BF16)
        out[d, base : base + rows.shape[0], :] = rows


def columns(arrived, table, w_in, weights, before, ranks, own, last):
    chans, hid = w_in.shape
    lat_rows = arrived.shape[1] // own
    waves = ranks * own
    slots = table.shape[1]
    points = 2 * slots
    together = 4
    rows_out = lat_rows // 2 * own
    lanes = 4 * chans
    if last:
        rows_out += (hid // lanes) * (2 * chans // ranks)
    sums = (2 * hid, 2 * chans + 16)
    after = (1, hid) if last else sums
    out_specs = [whole(ranks, rows_out, lanes), whole(*after)]
    out_shape = [
        jax.ShapeDtypeStruct((ranks, rows_out, lanes), BF16),
        jax.ShapeDtypeStruct(after, F32),
    ]
    sources = [arrived, table, w_in, weights] + before
    result = pl.pallas_call(
        functools.partial(column_kernel, ranks, own, not before, last),
        grid=(1,),
        in_specs=[HBM] * len(sources),
        out_specs=out_specs,
        out_shape=out_shape,
        scratch_shapes=[
            pltpu.VMEM(arrived.shape, BF16),
            pltpu.VMEM(table.shape, BF16),
            pltpu.VMEM(w_in.shape, BF16),
            pltpu.VMEM(weights.shape, BF16),
            pltpu.VMEM(sums, F32),
            pltpu.VMEM((2 * chans * lat_rows, 2 * waves), BF16),
            pltpu.VMEM((lat_rows, 2 * chans + 16, points), BF16),
            pltpu.VMEM((together, 2 * hid, points), BF16),
            pltpu.VMEM((lat_rows, chans, slots), BF16),
            pltpu.VMEM((lat_rows, chans, slots), BF16),
            pltpu.VMEM((lat_rows, chans, 128), BF16),
            pltpu.SemaphoreType.DMA((4 + slots // SLOTS,)),
        ],
        compiler_params=params(57),
        name="column_physics",
    )(*sources)
    return result[0], list(result[1:])


def backward_kernel(ranks, near, block, ahead, *refs):
    arrived_h, refs = refs[:PARTS], refs[PARTS:]
    cot_h, leg_h, damping_h, out_h = refs[:4]
    arrived, refs = refs[4 : 4 + PARTS], refs[4 + PARTS :]
    cot, leg, damping, out, rows, factor, in_sems, out_sems, sems = refs
    own, width, _ = cot.shape
    size = near * own
    early = copies_of([(damping_h, damping), *zip(arrived_h, arrived)], sems)

    def moves(c):
        here = pl.ds(c * block, block)
        return [
            pltpu.make_async_copy(src.at[here], dst.at[here], in_sems.at[c, k])
            for k, (src, dst) in enumerate(((cot_h, cot), (leg_h, leg)))
        ]

    def leave(c):
        here = pl.ds(c * block, block)
        return pltpu.make_async_copy(out.at[here], out_h.at[here], out_sems.at[c])

    for c in range(min(ahead, own // block)):
        for move in moves(c):
            move.start()
    early[0].wait()
    set_factor(factor, damping)
    for part in range(PARTS):
        early[1 + part].wait()
        for s in range(ranks):
            row = (part * ranks + s) * size
            rows[row : row + size, :] = arrived[part][s, :size, :].astype(F32)

    def step(c, carry):
        for move in moves(c):
            move.wait()

        @pl.when(c + ahead < own // block)
        def _():
            for move in moves(c + ahead):
                move.start()

        group = 2 if block % 2 == 0 else 1
        count = PARTS * ranks * near
        for k in range(0, block, group):
            members = [c * block + k + j for j in range(group)]
            mine = [rows[pl.ds(i, count, stride=own), :].astype(BF16) for i in members]
            mine = jnp.concatenate(mine, axis=0).T
            lhs = []
            for j in range(group):
                here = slice(j * count, (j + 1) * count)
                piece = jnp.concatenate([mine[:width, here], mine[width:, here]], axis=1)
                blank = jnp.zeros_like(piece)
                lhs.append(
                    jnp.concatenate([piece if g == j else blank for g in range(group)], axis=1)
                )
            product = dot_nt(
                jnp.concatenate(lhs, axis=0), jnp.concatenate([leg[i] for i in members], axis=1)
            )
            for j, i in enumerate(members):
                here = slice(j * width, (j + 1) * width)
                out[i] = cot[i].astype(F32) * factor[...] + product[here]
        leave(c).start()
        return carry

    lax.fori_loop(0, own // block, step, 0)
    for c in range(own // block):
        leave(c).wait()


def backward(arrived, cot, legendre, damping, ranks):
    own, width, degrees = cot.shape
    lat = legendre.shape[2]
    near = lat // ranks // 2 // PARTS
    block = block_of(own, 8)
    return pl.pallas_call(
        functools.partial(backward_kernel, ranks, near, block, 2),
        grid=(1,),
        in_specs=[HBM] * (PARTS + 3),
        out_specs=HBM,
        out_shape=jax.ShapeDtypeStruct((own, width, degrees), F32),
        scratch_shapes=[pltpu.VMEM(piece.shape, BF16) for piece in arrived]
        + [
            pltpu.VMEM(cot.shape, BF16),
            pltpu.VMEM(legendre.shape, BF16),
            pltpu.VMEM(damping.shape, F32),
            pltpu.VMEM(cot.shape, F32),
            pltpu.VMEM((PARTS * ranks * near * own, 2 * width), F32),
            pltpu.VMEM((width, degrees), F32),
            pltpu.SemaphoreType.DMA((own // block, 2)),
            pltpu.SemaphoreType.DMA((own // block,)),
            pltpu.SemaphoreType.DMA((PARTS + 1,)),
        ],
        compiler_params=params(57),
        name="legendre_backward",
    )(*arrived, cot, legendre, damping)


def collect_kernel(base, arrived, bias, out):
    lanes = arrived.shape[2]
    total = arrived[0, base:, :].astype(F32)
    for s in range(1, arrived.shape[0]):
        total = total + arrived[s, base:, :].astype(F32)
    cuts = range(0, bias.shape[1], lanes)
    total = jnp.concatenate([total] + [bias[:, c : c + lanes] for c in cuts], axis=0).astype(BF16)
    for s in range(out.shape[0]):
        out[s] = total


def collect(arrived, bias, base, copies):
    lanes = arrived.shape[2]
    shape = (copies, arrived.shape[1] - base + bias.shape[1] // lanes, lanes)
    return pl.pallas_call(
        functools.partial(collect_kernel, base),
        grid=(1,),
        in_specs=[whole(*arrived.shape), whole(*bias.shape)],
        out_specs=whole(*shape),
        out_shape=jax.ShapeDtypeStruct(shape, BF16),
        compiler_params=params(8),
        name="collect_gradients",
    )(arrived, bias)


def finish_kernel(groups, scale, parts, grad_in, grad_bias, grad_out):
    ranks = parts.shape[0] // groups
    chans, hid = grad_in.shape
    lanes = parts.shape[2]
    cuts = hid // lanes
    share = 2 * chans // ranks
    for r in range(ranks):
        total = parts[r].astype(F32)
        for g in range(1, groups):
            total = total + parts[g * ranks + r].astype(F32)
        total = total * scale
        row = r * share
        dest, row = (grad_in, row) if row < chans else (grad_out, row - chans)
        for c in range(cuts):
            dest[row : row + share, c * lanes : (c + 1) * lanes] = total[c * share : (c + 1) * share]
    tail = parts[0, cuts * share :].astype(F32)
    for s in range(1, parts.shape[0]):
        tail = tail + parts[s, cuts * share :].astype(F32)
    for c in range(cuts):
        grad_bias[:, c * lanes : (c + 1) * lanes] = tail[c : c + 1] * scale


def finish(parts, hid, chans, groups, scale):
    return pl.pallas_call(
        functools.partial(finish_kernel, groups, scale),
        grid=(1,),
        in_specs=[whole(*parts.shape)],
        out_specs=(whole(chans, hid), whole(1, hid), whole(chans, hid)),
        out_shape=(
            jax.ShapeDtypeStruct((chans, hid), F32),
            jax.ShapeDtypeStruct((1, hid), F32),
            jax.ShapeDtypeStruct((chans, hid), F32),
        ),
        compiler_params=params(8),
        name="weight_gradients",
    )(parts)


def body(
    spectral_state, cotangent, legendre, quadrature, damping, physics_in, physics_bias, physics_out
):
    spectral = spectral_state[0]
    cot = cotangent[0]
    own, width, degrees = spectral.shape
    chans = width // 2
    hid = physics_in.shape[0]
    ranks = lax.axis_size("lat")
    groups = lax.axis_size("grp")
    lat = legendre.shape[2]
    lat_rows = lat // ranks
    table = jnp.asarray(longitude_table(own * ranks, NLON))
    damping = damping[None, :]
    exchange = functools.partial(
        lax.all_to_all, axis_name="lat", split_axis=0, concat_axis=0, tiled=True
    )

    weights = column_weights(physics_in.T, physics_bias[None, :], physics_out)
    arrived = []
    for part in range(PARTS):
        sent = forward(spectral, cot, legendre, damping, quadrature[None, :], ranks, part)
        if arrived:
            sent, weights, arrived[-1] = lax.optimization_barrier((sent, weights, arrived[-1]))
        arrived.append(exchange(sent))
    sums = []
    returned = []
    for part in range(PARTS):
        back, sums = columns(
            arrived[part],
            table,
            physics_in.T,
            weights,
            sums,
            ranks,
            own,
            part == PARTS - 1,
        )
        if returned:
            back, returned[-1] = lax.optimization_barrier((back, returned[-1]))
        returned.append(exchange(back))

    base = lat_rows // 2 // PARTS * own
    spread = collect(returned[-1], sums[0], base, groups * ranks)
    parts = lax.all_to_all(spread, ("grp", "lat"), split_axis=0, concat_axis=0, tiled=True)
    grad_state = backward(returned, cot, legendre, damping, ranks)
    scale = 1.0 / math.sqrt(groups * lat * NLON)
    grad_in, grad_bias, grad_out = finish(parts, hid, chans, groups, scale)
    return (grad_state[None], grad_in.T, grad_bias[0], grad_out)


def solution(mesh):
    in_specs = (
        P("grp", "lat", None, None),
        P("grp", "lat", None, None),
        P("lat", None, None),
        P(),
        P(),
        P(),
        P(),
        P(),
    )
    out_specs = (P("grp", "lat", None, None), P(), P(), P())
    return jax.shard_map(body, mesh=mesh, in_specs=in_specs, out_specs=out_specs, check_vma=False)
```

profile of v0, /device:TPU:0, one launch (start us, length us, event | category | flops | bytes accessed | tf_op | source)
XLA Modules:
  0.0 113.8 jit_solution(15703797604861788731)
XLA Ops:
  0.6 7.3 %legendre_forward.3 = bf16[16,160,128]{2,1,0:T(8,128)(2,1)} custom-call(bf16[40,64,640]{2,1,0:T(8,128)(2,1)} %bitcast.12, bf16[40,64,640]{2,1,0:T(8,128)(2,1)} %bitcast.9, bf16[40,640,128]{2,1,0:T(8,128)(2,1)} %refs_3_.1, f32[1,32]{1,0:T(1,128)} %bitcast.18, f32[1,128]{1,0:T(1,128)} %bitcast.22), custom_call_target="tpu_custom_call" | custom-call | tf_op jit(solution)/shard_map/legendre_forward/pallas_call | solution.py:140
  7.9 8.3 %all-to-all-start = ((bf16[16,160,128]{2,1,0:T(8,128)(2,1)}), bf16[16,160,128]{2,1,0:T(8,128)(2,1)S(1)}, u32[]{:S(2)}, u32[]{:S(2)}) async-start(bf16[16,160,128]{2,1,0:T(8,128)(2,1)} %legendre_forward.3), calls=%async_computation | async-start | bytes 1310720 | tf_op jit(solution)/shard_map/all_to_all | solution.py:555
  16.2 7.3 %legendre_forward.2 = bf16[16,160,128]{2,1,0:T(8,128)(2,1)} custom-call(bf16[40,64,640]{2,1,0:T(8,128)(2,1)} %bitcast.13, bf16[40,64,640]{2,1,0:T(8,128)(2,1)} %bitcast.10, bf16[40,640,128]{2,1,0:T(8,128)(2,1)} %refs_3_.1, f32[1,32]{1,0:T(1,128)} %bitcast.19, f32[1,128]{1,0:T(1,128)} %bitcast.23), custom_call_target="tpu_custom_call" | custom-call | tf_op jit(solution)/shard_map/legendre_forward/pallas_call | solution.py:140
  23.5 1.6 %column_weights.1.refs_3_ = bf16[1024,80]{1,0:T(8,128)(2,1)} custom-call(bf16[32,512]{1,0:T(8,128)(2,1)} %bitcast.15, f32[1,512]{1,0:T(1,128)} %bitcast.21, bf16[32,512]{1,0:T(8,128)(2,1)} %w_out.1), custom_call_target="tpu_custom_call" | custom-call | tf_op jit(solution)/shard_map/column_weights/pallas_call | solution.py:191
  25.1 8.5 %all-to-all-done.refs_0_ = bf16[16,160,128]{2,1,0:T(8,128)(2,1)S(1)} async-done(((bf16[16,160,128]{2,1,0:T(8,128)(2,1)}), bf16[16,160,128]{2,1,0:T(8,128)(2,1)S(1)}, u32[]{:S(2)}, u32[]{:S(2)}) %all-to-all-start) | async-done | bytes 655392 | tf_op jit(solution)/shard_map/all_to_all | solution.py:555
  33.6 0.0 copy-start.3
  33.6 4.4 %all-to-all-start.1 = ((bf16[16,160,128]{2,1,0:T(8,128)(2,1)}), bf16[16,160,128]{2,1,0:T(8,128)(2,1)S(1)}, u32[]{:S(2)}, u32[]{:S(2)}) async-start(bf16[16,160,128]{2,1,0:T(8,128)(2,1)} %legendre_forward.2), calls=%async_computation.1 | async-start | bytes 1310720 | tf_op jit(solution)/shard_map/all_to_all | solution.py:555
  38.1 0.0 copy-done.3
  38.1 18.3 %column_physics.2 = (bf16[16,80,128]{2,1,0:T(8,128)(2,1)}, f32[1024,80]{1,0:T(8,128)}) custom-call(bf16[16,160,128]{2,1,0:T(8,128)(2,1)} %copy-done.3, bf16[1280,1280]{1,0:T(8,128)(2,1)} %constant.2.clone.refs_1_, bf16[32,512]{1,0:T(8,128)(2,1)} %bitcast.16, bf16[1024,80]{1,0:T(8,128)(2,1)} %column_weights.1.refs_3_), custom_call_target="tpu_custom_call" | custom-call | tf_op jit(solution)/shard_map/column_physics/pallas_call | solution.py:346
  56.4 0.0 all-to-all-done.1.refs_0_
  56.4 0.0 copy-start.2
  56.4 6.9 %all-to-all-start.2 = ((bf16[16,80,128]{2,1,0:T(8,128)(2,1)}), bf16[16,80,128]{2,1,0:T(8,128)(2,1)S(1)}, u32[]{:S(2)}, u32[]{:S(2)}) async-start(bf16[16,80,128]{2,1,0:T(8,128)(2,1)} %get-tuple-element.21), calls=%async_computation.2 | async-start | bytes 655360 | tf_op jit(solution)/shard_map/all_to_all | solution.py:571
  63.3 0.0 copy-done.2
  63.3 18.5 %column_physics.3 = (bf16[16,96,128]{2,1,0:T(8,128)(2,1)}, f32[1,512]{1,0:T(1,128)}) custom-call(bf16[16,160,128]{2,1,0:T(8,128)(2,1)} %copy-done.2, bf16[1280,1280]{1,0:T(8,128)(2,1)} %constant.2.clone.refs_1_, bf16[32,512]{1,0:T(8,128)(2,1)} %bitcast.17, bf16[1024,80]{1,0:T(8,128)(2,1)} %column_weights.1.refs_3_, f32[1024,80]{1,0:T(8,128)} %get-tuple-element.19.refs_4_), custom_call_target="tpu_custom_call" | custom-call | tf_op jit(solution)/shard_map/column_physics/pallas_call | solution.py:346
  81.8 0.0 all-to-all-done.2.refs_0_
  81.8 0.0 copy-start.4
  81.8 17.2 %all_to_all.25.refs_1_.arrived = bf16[16,96,128]{2,1,0:T(8,128)(2,1)S(1)} all-to-all(bf16[16,96,128]{2,1,0:T(8,128)(2,1)} %get-tuple-element.23), channel_id=1, replica_groups=mesh['grp'=2,'lat'=16] {'lat'}, dimensions={0} | all-to-all | bytes 786432 | tf_op jit(solution)/shard_map/all_to_all | solution.py:571
  99.0 0.0 copy-start
  99.0 0.0 copy-start.1
  99.0 0.7 copy-done.1
  99.7 0.7 collect_gradients.1
  100.4 2.9 %all-to-all-start.4 = ((bf16[32,20,128]{2,1,0:T(8,128)(2,1)}), bf16[32,20,128]{2,1,0:T(8,128)(2,1)S(1)}, u32[]{:S(2)}, u32[]{:S(2)}) async-start(bf16[32,20,128]{2,1,0:T(8,128)(2,1)} %collect_gradients.1), calls=%async_computation.4 | async-start | bytes 393216 | tf_op jit(solution)/shard_map/all_to_all | solution.py:575
  103.3 0.0 copy-done.4
  103.3 0.0 copy-done
  103.3 7.9 %legendre_backward.1 = f32[40,64,640]{2,1,0:T(8,128)} custom-call(bf16[16,80,128]{2,1,0:T(8,128)(2,1)} %copy-done.4, bf16[16,96,128]{2,1,0:T(8,128)(2,1)} %copy-done, bf16[40,64,640]{2,1,0:T(8,128)(2,1)} %bitcast.11, bf16[40,640,128]{2,1,0:T(8,128)(2,1)} %refs_3_.1, f32[1,32]{1,0:T(1,128)} %bitcast.20), custom_call_target="tpu_custom_call" | custom-call | tf_op jit(solution)/shard_map/legendre_backward/pallas_call | solution.py:445
  111.3 1.8 %all-to-all-done.4.parts = bf16[32,20,128]{2,1,0:T(8,128)(2,1)S(1)} async-done(((bf16[32,20,128]{2,1,0:T(8,128)(2,1)}), bf16[32,20,128]{2,1,0:T(8,128)(2,1)S(1)}, u32[]{:S(2)}, u32[]{:S(2)}) %all-to-all-start.4) | async-done | bytes 163872 | tf_op jit(solution)/shard_map/all_to_all | solution.py:575
  113.1 0.7 weight_gradients.1
Async XLA Ops:
  7.9 25.8 %all-to-all-start = ((bf16[16,160,128]{2,1,0:T(8,128)(2,1)}), bf16[16,160,128]{2,1,0:T(8,128)(2,1)S(1)}, u32[]{:S(2)}, u32[]{:S(2)}) async-start(bf16[16,160,128]{2,1,0:T(8,128)(2,1)} %legendre_forward.3), calls=%async_computation | async-start | bytes 1310720 | tf_op jit(solution)/shard_map/all_to_all | solution.py:555
  33.6 4.4 %copy-start.3 = (bf16[16,160,128]{2,1,0:T(8,128)(2,1)}, bf16[16,160,128]{2,1,0:T(8,128)(2,1)S(1)}, u32[]{:S(2)}) copy-start(bf16[16,160,128]{2,1,0:T(8,128)(2,1)S(1)} %all-to-all-done.refs_0_) | copy-start | bytes 1966084
  33.6 22.7 %all-to-all-start.1 = ((bf16[16,160,128]{2,1,0:T(8,128)(2,1)}), bf16[16,160,128]{2,1,0:T(8,128)(2,1)S(1)}, u32[]{:S(2)}, u32[]{:S(2)}) async-start(bf16[16,160,128]{2,1,0:T(8,128)(2,1)} %legendre_forward.2), calls=%async_computation.1 | async-start | bytes 1310720 | tf_op jit(solution)/shard_map/all_to_all | solution.py:555
  56.4 6.9 %copy-start.2 = (bf16[16,160,128]{2,1,0:T(8,128)(2,1)}, bf16[16,160,128]{2,1,0:T(8,128)(2,1)S(1)}, u32[]{:S(2)}) copy-start(bf16[16,160,128]{2,1,0:T(8,128)(2,1)S(1)} %all-to-all-done.1.refs_0_) | copy-start | bytes 1966084
  56.4 25.4 %all-to-all-start.2 = ((bf16[16,80,128]{2,1,0:T(8,128)(2,1)}), bf16[16,80,128]{2,1,0:T(8,128)(2,1)S(1)}, u32[]{:S(2)}, u32[]{:S(2)}) async-start(bf16[16,80,128]{2,1,0:T(8,128)(2,1)} %get-tuple-element.21), calls=%async_computation.2 | async-start | bytes 655360 | tf_op jit(solution)/shard_map/all_to_all | solution.py:571
  81.8 21.5 %copy-start.4 = (bf16[16,80,128]{2,1,0:T(8,128)(2,1)}, bf16[16,80,128]{2,1,0:T(8,128)(2,1)S(1)}, u32[]{:S(2)}) copy-start(bf16[16,80,128]{2,1,0:T(8,128)(2,1)S(1)} %all-to-all-done.2.refs_0_) | copy-start | bytes 983044
  99.0 4.3 %copy-start = (bf16[16,96,128]{2,1,0:T(8,128)(2,1)}, bf16[16,96,128]{2,1,0:T(8,128)(2,1)S(1)}, u32[]{:S(2)}) copy-start(bf16[16,96,128]{2,1,0:T(8,128)(2,1)S(1)} %all_to_all.25.refs_1_.arrived) | copy-start | bytes 1179652
  99.0 0.7 copy-start.1
  100.4 12.7 %all-to-all-start.4 = ((bf16[32,20,128]{2,1,0:T(8,128)(2,1)}), bf16[32,20,128]{2,1,0:T(8,128)(2,1)S(1)}, u32[]{:S(2)}, u32[]{:S(2)}) async-start(bf16[32,20,128]{2,1,0:T(8,128)(2,1)} %collect_gradients.1), calls=%async_computation.4 | async-start | bytes 393216 | tf_op jit(solution)/shard_map/all_to_all | solution.py:575
where the time goes:
time: 115 us; the launch traced here: 114 us
  Pallas kernels  62.2 us (54%)
  starting transfers between devices  22.5 us (20%)
  blocking collectives  17.2 us (15%)
  waiting for transfers between devices  10.4 us (9%)
    pallas_call x2, Pallas kernels, columns(): pl.pallas_call(functools.partial(column_kernel, ranks, own, not before, l...  36.7 us
    all_to_all x1, blocking collectives, body(): returned.append(exchange(back))  17.2 us
    pallas_call x2, Pallas kernels, forward(): pl.pallas_call(functools.partial(forward_kernel, ranks, block, part), gri...  14.5 us
    all_to_all x2, starting transfers between devices, body(): arrived.append(exchange(sent))  12.7 us
    all_to_all x2, waiting for transfers between devices, body(): arrived.append(exchange(sent))  8.52 us
    pallas_call x1, Pallas kernels, backward(): pl.pallas_call(functools.partial(backward_kernel, ranks, near, block, 2),...  7.94 us
    all_to_all x1, starting transfers between devices, body(): returned.append(exchange(back))  6.92 us
    all_to_all x1, starting transfers between devices, body(): lax.all_to_all(spread, ('grp', 'lat'), split_axis=0, concat_axis=0, tiled...  2.87 us
  transfers between devices with their start and end apart: 4, of which 2 were waited for; matrix products, arithmetic and copies ran while one was open for 0% of the time, Pallas kernels for 47%

commit v1 on v0

--- a/solution.py
+++ b/solution.py
@@ -85,8 +85,7 @@
             for k, (src, dst) in enumerate(((spec_h, spec), (cot_h, cot), (leg_h, leg)))
         ]
 
-    ahead = 4
-    for c in range(min(ahead, own // block)):
+    for c in range(own // block):
         for move in moves(c):
             move.start()
     set_factor(factor, damping)
@@ -94,12 +93,6 @@
     def step(c, carry):
         for move in moves(c):
             move.wait()
-
-        @pl.when(c + ahead < own // block)
-        def _():
-            for move in moves(c + ahead):
-                move.start()
-
         weight = quad[...]
         for k in range(block):
             i = c * block + k
@@ -135,7 +128,7 @@
 def forward(spectral, cot, legendre, damping, quad, ranks, part):
     own, width, degrees = spectral.shape
     lat = legendre.shape[2]
-    block = block_of(own, 4)
+    block = block_of(own, 8)
     shape = (ranks, lat // ranks // PARTS * own, 2 * width)
     return pl.pallas_call(
         functools.partial(forward_kernel, ranks, block, part),
@@ -225,13 +218,11 @@
         moves.append(
             pltpu.make_async_copy(table_h.at[:, here], table.at[:, here], sems.at[4 + c])
         )
-    moves[0].start()
+        moves[c].start()
     for p in range(lat_rows):
         cols[p, width:, :] = jnp.ones((16, points), BF16)
     for copy in small:
         copy.wait()
-    for move in moves[1:]:
-        move.start()
     if first:
         sums[...] = jnp.zeros_like(sums)
     for p in range(lat_rows):

time: 115 us -> 113 us (0.983)
  Pallas kernels: 62.2 us -> 60.9 us
where the time goes in v1:
time: 113 us
  Pallas kernels  60.9 us (54%)
  starting transfers between devices  22.5 us (20%)
  blocking collectives  17.2 us (15%)
  waiting for transfers between devices  10.6 us (9%)
    pallas_call x2, Pallas kernels, columns(): pl.pallas_call(functools.partial(column_kernel, ranks, own, not before, l...  35.9 us
    all_to_all x1, blocking collectives, body(): returned.append(exchange(back))  17.2 us
    pallas_call x2, Pallas kernels, forward(): pl.pallas_call(functools.partial(forward_kernel, ranks, block, part), gri...  14.1 us
    all_to_all x2, starting transfers between devices, body(): arrived.append(exchange(sent))  12.7 us
    all_to_all x2, waiting for transfers between devices, body(): arrived.append(exchange(sent))  8.75 us
    pallas_call x1, Pallas kernels, backward(): pl.pallas_call(functools.partial(backward_kernel, ranks, near, block, 2),...  7.94 us
    all_to_all x1, starting transfers between devices, body(): returned.append(exchange(back))  6.92 us
    all_to_all x1, starting transfers between devices, body(): lax.all_to_all(spread, ('grp', 'lat'), split_axis=0, concat_axis=0, tiled...  2.87 us
  transfers between devices with their start and end apart: 4, of which 2 were waited for; matrix products, arithmetic and copies ran while one was open for 0% of the time, Pallas kernels for 47%

profile of v1, /device:TPU:0, one launch (start us, length us, event | category | flops | bytes accessed | tf_op | source)
XLA Modules:
  0.0 112.7 jit_solution(13513523996101947659)
XLA Ops:
  0.6 7.0 %legendre_forward.3 = bf16[16,160,128]{2,1,0:T(8,128)(2,1)} custom-call(bf16[40,64,640]{2,1,0:T(8,128)(2,1)} %bitcast.12, bf16[40,64,640]{2,1,0:T(8,128)(2,1)} %bitcast.9, bf16[40,640,128]{2,1,0:T(8,128)(2,1)} %refs_3_.1, f32[1,32]{1,0:T(1,128)} %bitcast.18, f32[1,128]{1,0:T(1,128)} %bitcast.22), custom_call_target="tpu_custom_call" | custom-call | tf_op jit(solution)/shard_map/legendre_forward/pallas_call | solution.py:133
  7.7 8.3 %all-to-all-start = ((bf16[16,160,128]{2,1,0:T(8,128)(2,1)}), bf16[16,160,128]{2,1,0:T(8,128)(2,1)S(1)}, u32[]{:S(2)}, u32[]{:S(2)}) async-start(bf16[16,160,128]{2,1,0:T(8,128)(2,1)} %legendre_forward.3), calls=%async_computation | async-start | bytes 1310720 | tf_op jit(solution)/shard_map/all_to_all | solution.py:546
  16.0 7.0 %legendre_forward.2 = bf16[16,160,128]{2,1,0:T(8,128)(2,1)} custom-call(bf16[40,64,640]{2,1,0:T(8,128)(2,1)} %bitcast.13, bf16[40,64,640]{2,1,0:T(8,128)(2,1)} %bitcast.10, bf16[40,640,128]{2,1,0:T(8,128)(2,1)} %refs_3_.1, f32[1,32]{1,0:T(1,128)} %bitcast.19, f32[1,128]{1,0:T(1,128)} %bitcast.23), custom_call_target="tpu_custom_call" | custom-call | tf_op jit(solution)/shard_map/legendre_forward/pallas_call | solution.py:133
  23.1 1.6 %column_weights.1.refs_3_ = bf16[1024,80]{1,0:T(8,128)(2,1)} custom-call(bf16[32,512]{1,0:T(8,128)(2,1)} %bitcast.15, f32[1,512]{1,0:T(1,128)} %bitcast.21, bf16[32,512]{1,0:T(8,128)(2,1)} %w_out.1), custom_call_target="tpu_custom_call" | custom-call | tf_op jit(solution)/shard_map/column_weights/pallas_call | solution.py:184
  24.7 8.7 %all-to-all-done.refs_0_ = bf16[16,160,128]{2,1,0:T(8,128)(2,1)S(1)} async-done(((bf16[16,160,128]{2,1,0:T(8,128)(2,1)}), bf16[16,160,128]{2,1,0:T(8,128)(2,1)S(1)}, u32[]{:S(2)}, u32[]{:S(2)}) %all-to-all-start) | async-done | bytes 655392 | tf_op jit(solution)/shard_map/all_to_all | solution.py:546
  33.4 0.0 copy-start.3
  33.4 4.4 %all-to-all-start.1 = ((bf16[16,160,128]{2,1,0:T(8,128)(2,1)}), bf16[16,160,128]{2,1,0:T(8,128)(2,1)S(1)}, u32[]{:S(2)}, u32[]{:S(2)}) async-start(bf16[16,160,128]{2,1,0:T(8,128)(2,1)} %legendre_forward.2), calls=%async_computation.1 | async-start | bytes 1310720 | tf_op jit(solution)/shard_map/all_to_all | solution.py:546
  37.8 0.0 copy-done.3
  37.9 17.9 %column_physics.2 = (bf16[16,80,128]{2,1,0:T(8,128)(2,1)}, f32[1024,80]{1,0:T(8,128)}) custom-call(bf16[16,160,128]{2,1,0:T(8,128)(2,1)} %copy-done.3, bf16[1280,1280]{1,0:T(8,128)(2,1)} %constant.2.clone.refs_1_, bf16[32,512]{1,0:T(8,128)(2,1)} %bitcast.16, bf16[1024,80]{1,0:T(8,128)(2,1)} %column_weights.1.refs_3_), custom_call_target="tpu_custom_call" | custom-call | tf_op jit(solution)/shard_map/column_physics/pallas_call | solution.py:337
  55.7 0.0 all-to-all-done.1.refs_0_
  55.7 0.0 copy-start.2
  55.7 6.9 %all-to-all-start.2 = ((bf16[16,80,128]{2,1,0:T(8,128)(2,1)}), bf16[16,80,128]{2,1,0:T(8,128)(2,1)S(1)}, u32[]{:S(2)}, u32[]{:S(2)}) async-start(bf16[16,80,128]{2,1,0:T(8,128)(2,1)} %get-tuple-element.21), calls=%async_computation.2 | async-start | bytes 655360 | tf_op jit(solution)/shard_map/all_to_all | solution.py:562
  62.7 0.0 copy-done.2
  62.7 18.1 %column_physics.3 = (bf16[16,96,128]{2,1,0:T(8,128)(2,1)}, f32[1,512]{1,0:T(1,128)}) custom-call(bf16[16,160,128]{2,1,0:T(8,128)(2,1)} %copy-done.2, bf16[1280,1280]{1,0:T(8,128)(2,1)} %constant.2.clone.refs_1_, bf16[32,512]{1,0:T(8,128)(2,1)} %bitcast.17, bf16[1024,80]{1,0:T(8,128)(2,1)} %column_weights.1.refs_3_, f32[1024,80]{1,0:T(8,128)} %get-tuple-element.19.refs_4_), custom_call_target="tpu_custom_call" | custom-call | tf_op jit(solution)/shard_map/column_physics/pallas_call | solution.py:337
  80.7 0.0 all-to-all-done.2.refs_0_
  80.8 0.0 copy-start.4
  80.8 17.2 %all_to_all.25.refs_1_.arrived = bf16[16,96,128]{2,1,0:T(8,128)(2,1)S(1)} all-to-all(bf16[16,96,128]{2,1,0:T(8,128)(2,1)} %get-tuple-element.23), channel_id=1, replica_groups=mesh['grp'=2,'lat'=16] {'lat'}, dimensions={0} | all-to-all | bytes 786432 | tf_op jit(solution)/shard_map/all_to_all | solution.py:562
  98.0 0.0 copy-start
  98.0 0.0 copy-start.1
  98.0 0.7 copy-done.1
  98.6 0.7 collect_gradients.1
  99.3 2.9 %all-to-all-start.4 = ((bf16[32,20,128]{2,1,0:T(8,128)(2,1)}), bf16[32,20,128]{2,1,0:T(8,128)(2,1)S(1)}, u32[]{:S(2)}, u32[]{:S(2)}) async-start(bf16[32,20,128]{2,1,0:T(8,128)(2,1)} %collect_gradients.1), calls=%async_computation.4 | async-start | bytes 393216 | tf_op jit(solution)/shard_map/all_to_all | solution.py:566
  102.2 0.0 copy-done.4
  102.2 0.0 copy-done
  102.2 7.9 %legendre_backward.1 = f32[40,64,640]{2,1,0:T(8,128)} custom-call(bf16[16,80,128]{2,1,0:T(8,128)(2,1)} %copy-done.4, bf16[16,96,128]{2,1,0:T(8,128)(2,1)} %copy-done, bf16[40,64,640]{2,1,0:T(8,128)(2,1)} %bitcast.11, bf16[40,640,128]{2,1,0:T(8,128)(2,1)} %refs_3_.1, f32[1,32]{1,0:T(1,128)} %bitcast.20), custom_call_target="tpu_custom_call" | custom-call | tf_op jit(solution)/shard_map/legendre_backward/pallas_call | solution.py:436
  110.2 1.8 %all-to-all-done.4.parts = bf16[32,20,128]{2,1,0:T(8,128)(2,1)S(1)} async-done(((bf16[32,20,128]{2,1,0:T(8,128)(2,1)}), bf16[32,20,128]{2,1,0:T(8,128)(2,1)S(1)}, u32[]{:S(2)}, u32[]{:S(2)}) %all-to-all-start.4) | async-done | bytes 163872 | tf_op jit(solution)/shard_map/all_to_all | solution.py:566
  112.0 0.7 weight_gradients.1
Async XLA Ops:
  7.7 25.7 %all-to-all-start = ((bf16[16,160,128]{2,1,0:T(8,128)(2,1)}), bf16[16,160,128]{2,1,0:T(8,128)(2,1)S(1)}, u32[]{:S(2)}, u32[]{:S(2)}) async-start(bf16[16,160,128]{2,1,0:T(8,128)(2,1)} %legendre_forward.3), calls=%async_computation | async-start | bytes 1310720 | tf_op jit(solution)/shard_map/all_to_all | solution.py:546
  33.4 4.4 %copy-start.3 = (bf16[16,160,128]{2,1,0:T(8,128)(2,1)}, bf16[16,160,128]{2,1,0:T(8,128)(2,1)S(1)}, u32[]{:S(2)}) copy-start(bf16[16,160,128]{2,1,0:T(8,128)(2,1)S(1)} %all-to-all-done.refs_0_) | copy-start | bytes 1966084
  33.4 22.3 %all-to-all-start.1 = ((bf16[16,160,128]{2,1,0:T(8,128)(2,1)}), bf16[16,160,128]{2,1,0:T(8,128)(2,1)S(1)}, u32[]{:S(2)}, u32[]{:S(2)}) async-start(bf16[16,160,128]{2,1,0:T(8,128)(2,1)} %legendre_forward.2), calls=%async_computation.1 | async-start | bytes 1310720 | tf_op jit(solution)/shard_map/all_to_all | solution.py:546
  55.7 6.9 %copy-start.2 = (bf16[16,160,128]{2,1,0:T(8,128)(2,1)}, bf16[16,160,128]{2,1,0:T(8,128)(2,1)S(1)}, u32[]{:S(2)}) copy-start(bf16[16,160,128]{2,1,0:T(8,128)(2,1)S(1)} %all-to-all-done.1.refs_0_) | copy-start | bytes 1966084
  55.7 25.0 %all-to-all-start.2 = ((bf16[16,80,128]{2,1,0:T(8,128)(2,1)}), bf16[16,80,128]{2,1,0:T(8,128)(2,1)S(1)}, u32[]{:S(2)}, u32[]{:S(2)}) async-start(bf16[16,80,128]{2,1,0:T(8,128)(2,1)} %get-tuple-element.21), calls=%async_computation.2 | async-start | bytes 655360 | tf_op jit(solution)/shard_map/all_to_all | solution.py:562
  80.8 21.5 %copy-start.4 = (bf16[16,80,128]{2,1,0:T(8,128)(2,1)}, bf16[16,80,128]{2,1,0:T(8,128)(2,1)S(1)}, u32[]{:S(2)}) copy-start(bf16[16,80,128]{2,1,0:T(8,128)(2,1)S(1)} %all-to-all-done.2.refs_0_) | copy-start | bytes 983044
  98.0 4.3 %copy-start = (bf16[16,96,128]{2,1,0:T(8,128)(2,1)}, bf16[16,96,128]{2,1,0:T(8,128)(2,1)S(1)}, u32[]{:S(2)}) copy-start(bf16[16,96,128]{2,1,0:T(8,128)(2,1)S(1)} %all_to_all.25.refs_1_.arrived) | copy-start | bytes 1179652
  98.0 0.7 copy-start.1
  99.3 12.7 %all-to-all-start.4 = ((bf16[32,20,128]{2,1,0:T(8,128)(2,1)}), bf16[32,20,128]{2,1,0:T(8,128)(2,1)S(1)}, u32[]{:S(2)}, u32[]{:S(2)}) async-start(bf16[32,20,128]{2,1,0:T(8,128)(2,1)} %collect_gradients.1), calls=%async_computation.4 | async-start | bytes 393216 | tf_op jit(solution)/shard_map/all_to_all | solution.py:566

commit v2 on v1

--- a/solution.py
+++ b/solution.py
@@ -16,7 +16,7 @@
 BF16 = jnp.bfloat16
 PARTS = 2
 SLOTS = 256
-UNIT = 128
+UNIT = 256
 HBM = pl.BlockSpec(memory_space=pl.ANY)
 
 
@@ -254,35 +254,34 @@
             cols[p, :width, here] = front[width * p : width * (p + 1)]
             cols[p, :width, there] = rear[width * p : width * (p + 1)]
 
-    together = acts.shape[0]
-    span = 512
-
-    def rows_step(g, carry):
-        for r in range(together):
-            p = g * together + r
-            for n in range(0, points, span):
-                here = slice(n, n + span)
-                columns_here = cols[p, :, here]
-                for k in range(0, hid, UNIT):
-                    both = dot(weights[2 * k : 2 * k + 2 * UNIT, :], columns_here).astype(BF16)
-                    arg = both[:UNIT]
-                    th = jnp.tanh(arg)
-                    rise = 1 + th
-                    act = arg * rise
-                    acts[r, k : k + UNIT, here] = act
-                    acts[r, hid + k : hid + k + UNIT, here] = both[UNIT:] * (
-                        rise + act * (1 - th)
-                    )
-            grad = dot(w_in[...], acts[r, hid:, :])
-            front, rear = grad[:, :slots], grad[:, slots:]
-            edge[p] = rear[:, :128].astype(BF16)
-            slot = lax.broadcasted_iota(jnp.int32, rear.shape, 1)
-            evens[p] = (front + jnp.where(slot == 0, 0.0, rear)).astype(BF16)
-            odds[p] = (front - rear).astype(BF16)
-            sums[...] += dot_nt(acts[r], cols[p])
-        return carry
-
-    lax.fori_loop(0, lat_rows // together, rows_step, 0)
+    steps = [(p, n) for p in range(lat_rows) for n in range(2)]
+    front = None
+    for at in range(len(steps) + 1):
+        for k in range(0, hid, UNIT):
+            if at < len(steps):
+                p, n = steps[at]
+                here = slice(n * slots, (n + 1) * slots)
+                both = dot(weights[2 * k : 2 * k + 2 * UNIT, :], cols[p, :, here]).astype(BF16)
+                arg = both[:UNIT]
+                th = jnp.tanh(arg)
+                rise = 1 + th
+                act = arg * rise
+                acts[p, k : k + UNIT, here] = act
+                acts[p, hid + k : hid + k + UNIT, here] = both[UNIT:] * (rise + act * (1 - th))
+            if at > 0:
+                p, n = steps[at - 1]
+                here = slice(n * slots, (n + 1) * slots)
+                some = slice(2 * k, 2 * k + 2 * UNIT)
+                sums[some, :] += dot_nt(acts[p, some, here], cols[p, :, here])
+        if at > 0:
+            grad = dot(w_in[...], acts[p, hid:, here])
+            if n == 0:
+                front = grad
+            else:
+                edge[p] = grad[:, :128].astype(BF16)
+                slot = lax.broadcasted_iota(jnp.int32, grad.shape, 1)
+                evens[p] = (front + jnp.where(slot == 0, 0.0, grad)).astype(BF16)
+                odds[p] = (front - grad).astype(BF16)
 
     def joined(ref):
         return ref[...].reshape(chans * lat_rows, ref.shape[2])
@@ -321,7 +320,6 @@
     waves = ranks * own
     slots = table.shape[1]
     points = 2 * slots
-    together = 4
     rows_out = lat_rows // 2 * own
     lanes = 4 * chans
     if last:
@@ -348,7 +346,7 @@
             pltpu.VMEM(sums, F32),
             pltpu.VMEM((2 * chans * lat_rows, 2 * waves), BF16),
             pltpu.VMEM((lat_rows, 2 * chans + 16, points), BF16),
-            pltpu.VMEM((together, 2 * hid, points), BF16),
+            pltpu.VMEM((lat_rows, 2 * hid, points), BF16),
             pltpu.VMEM((lat_rows, chans, slots), BF16),
             pltpu.VMEM((lat_rows, chans, slots), BF16),
             pltpu.VMEM((lat_rows, chans, 128), BF16),

time: 113 us -> 114 us (level)
  no operation moved by 1% of the time
where the time goes in v2:
time: 114 us; the launch traced here: 113 us
  Pallas kernels  61.2 us (54%)
  starting transfers between devices  22.5 us (20%)
  blocking collectives  17.2 us (15%)
  waiting for transfers between devices  10.6 us (9%)
    pallas_call x2, Pallas kernels, columns(): pl.pallas_call(functools.partial(column_kernel, ranks, own, not before, l...  36.2 us
    all_to_all x1, blocking collectives, body(): returned.append(exchange(back))  17.2 us
    pallas_call x2, Pallas kernels, forward(): pl.pallas_call(functools.partial(forward_kernel, ranks, block, part), gri...  14.1 us
    all_to_all x2, starting transfers between devices, body(): arrived.append(exchange(sent))  12.7 us
    all_to_all x2, waiting for transfers between devices, body(): arrived.append(exchange(sent))  8.75 us
    pallas_call x1, Pallas kernels, backward(): pl.pallas_call(functools.partial(backward_kernel, ranks, near, block, 2),...  7.94 us
    all_to_all x1, starting transfers between devices, body(): returned.append(exchange(back))  6.92 us
    all_to_all x1, starting transfers between devices, body(): lax.all_to_all(spread, ('grp', 'lat'), split_axis=0, concat_axis=0, tiled...  2.87 us
  transfers between devices with their start and end apart: 4, of which 2 were waited for; matrix products, arithmetic and copies ran while one was open for 0% of the time, Pallas kernels for 47%

profile of v2, /device:TPU:0, one launch (start us, length us, event | category | flops | bytes accessed | tf_op | source)
XLA Modules:
  0.0 113.0 jit_solution(14237679190935543582)
XLA Ops:
  0.6 7.0 %legendre_forward.3 = bf16[16,160,128]{2,1,0:T(8,128)(2,1)} custom-call(bf16[40,64,640]{2,1,0:T(8,128)(2,1)} %bitcast.12, bf16[40,64,640]{2,1,0:T(8,128)(2,1)} %bitcast.9, bf16[40,640,128]{2,1,0:T(8,128)(2,1)} %refs_3_.1, f32[1,32]{1,0:T(1,128)} %bitcast.18, f32[1,128]{1,0:T(1,128)} %bitcast.22), custom_call_target="tpu_custom_call" | custom-call | tf_op jit(solution)/shard_map/legendre_forward/pallas_call | solution.py:133
  7.7 8.3 %all-to-all-start = ((bf16[16,160,128]{2,1,0:T(8,128)(2,1)}), bf16[16,160,128]{2,1,0:T(8,128)(2,1)S(1)}, u32[]{:S(2)}, u32[]{:S(2)}) async-start(bf16[16,160,128]{2,1,0:T(8,128)(2,1)} %legendre_forward.3), calls=%async_computation | async-start | bytes 1310720 | tf_op jit(solution)/shard_map/all_to_all | solution.py:544
  16.0 7.0 %legendre_forward.2 = bf16[16,160,128]{2,1,0:T(8,128)(2,1)} custom-call(bf16[40,64,640]{2,1,0:T(8,128)(2,1)} %bitcast.13, bf16[40,64,640]{2,1,0:T(8,128)(2,1)} %bitcast.10, bf16[40,640,128]{2,1,0:T(8,128)(2,1)} %refs_3_.1, f32[1,32]{1,0:T(1,128)} %bitcast.19, f32[1,128]{1,0:T(1,128)} %bitcast.23), custom_call_target="tpu_custom_call" | custom-call | tf_op jit(solution)/shard_map/legendre_forward/pallas_call | solution.py:133
  23.1 1.6 %column_weights.1.refs_3_ = bf16[1024,80]{1,0:T(8,128)(2,1)} custom-call(bf16[32,512]{1,0:T(8,128)(2,1)} %bitcast.15, f32[1,512]{1,0:T(1,128)} %bitcast.21, bf16[32,512]{1,0:T(8,128)(2,1)} %w_out.1), custom_call_target="tpu_custom_call" | custom-call | tf_op jit(solution)/shard_map/column_weights/pallas_call | solution.py:184
  24.7 8.7 %all-to-all-done.refs_0_ = bf16[16,160,128]{2,1,0:T(8,128)(2,1)S(1)} async-done(((bf16[16,160,128]{2,1,0:T(8,128)(2,1)}), bf16[16,160,128]{2,1,0:T(8,128)(2,1)S(1)}, u32[]{:S(2)}, u32[]{:S(2)}) %all-to-all-start) | async-done | bytes 655392 | tf_op jit(solution)/shard_map/all_to_all | solution.py:544
  33.4 0.0 copy-start.3
  33.4 4.4 %all-to-all-start.1 = ((bf16[16,160,128]{2,1,0:T(8,128)(2,1)}), bf16[16,160,128]{2,1,0:T(8,128)(2,1)S(1)}, u32[]{:S(2)}, u32[]{:S(2)}) async-start(bf16[16,160,128]{2,1,0:T(8,128)(2,1)} %legendre_forward.2), calls=%async_computation.1 | async-start | bytes 1310720 | tf_op jit(solution)/shard_map/all_to_all | solution.py:544
  37.8 0.0 copy-done.3
  37.9 18.0 %column_physics.2 = (bf16[16,80,128]{2,1,0:T(8,128)(2,1)}, f32[1024,80]{1,0:T(8,128)}) custom-call(bf16[16,160,128]{2,1,0:T(8,128)(2,1)} %copy-done.3, bf16[1280,1280]{1,0:T(8,128)(2,1)} %constant.2.clone.refs_1_, bf16[32,512]{1,0:T(8,128)(2,1)} %bitcast.16, bf16[1024,80]{1,0:T(8,128)(2,1)} %column_weights.1.refs_3_), custom_call_target="tpu_custom_call" | custom-call | tf_op jit(solution)/shard_map/column_physics/pallas_call | solution.py:335
  55.8 0.0 all-to-all-done.1.refs_0_
  55.9 0.0 copy-start.2
  55.9 6.9 %all-to-all-start.2 = ((bf16[16,80,128]{2,1,0:T(8,128)(2,1)}), bf16[16,80,128]{2,1,0:T(8,128)(2,1)S(1)}, u32[]{:S(2)}, u32[]{:S(2)}) async-start(bf16[16,80,128]{2,1,0:T(8,128)(2,1)} %get-tuple-element.21), calls=%async_computation.2 | async-start | bytes 655360 | tf_op jit(solution)/shard_map/all_to_all | solution.py:560
  62.8 0.0 copy-done.2
  62.8 18.2 %column_physics.3 = (bf16[16,96,128]{2,1,0:T(8,128)(2,1)}, f32[1,512]{1,0:T(1,128)}) custom-call(bf16[16,160,128]{2,1,0:T(8,128)(2,1)} %copy-done.2, bf16[1280,1280]{1,0:T(8,128)(2,1)} %constant.2.clone.refs_1_, bf16[32,512]{1,0:T(8,128)(2,1)} %bitcast.17, bf16[1024,80]{1,0:T(8,128)(2,1)} %column_weights.1.refs_3_, f32[1024,80]{1,0:T(8,128)} %get-tuple-element.19.refs_4_), custom_call_target="tpu_custom_call" | custom-call | tf_op jit(solution)/shard_map/column_physics/pallas_call | solution.py:335
  81.0 0.0 all-to-all-done.2.refs_0_
  81.0 0.0 copy-start.4
  81.0 17.2 %all_to_all.25.refs_1_.arrived = bf16[16,96,128]{2,1,0:T(8,128)(2,1)S(1)} all-to-all(bf16[16,96,128]{2,1,0:T(8,128)(2,1)} %get-tuple-element.23), channel_id=1, replica_groups=mesh['grp'=2,'lat'=16] {'lat'}, dimensions={0} | all-to-all | bytes 786432 | tf_op jit(solution)/shard_map/all_to_all | solution.py:560
  98.2 0.0 copy-start
  98.2 0.0 copy-start.1
  98.2 0.7 copy-done.1
  98.9 0.7 collect_gradients.1
  99.6 2.9 %all-to-all-start.4 = ((bf16[32,20,128]{2,1,0:T(8,128)(2,1)}), bf16[32,20,128]{2,1,0:T(8,128)(2,1)S(1)}, u32[]{:S(2)}, u32[]{:S(2)}) async-start(bf16[32,20,128]{2,1,0:T(8,128)(2,1)} %collect_gradients.1), calls=%async_computation.4 | async-start | bytes 393216 | tf_op jit(solution)/shard_map/all_to_all | solution.py:564
  102.5 0.0 copy-done.4
  102.5 0.0 copy-done
  102.5 7.9 %legendre_backward.1 = f32[40,64,640]{2,1,0:T(8,128)} custom-call(bf16[16,80,128]{2,1,0:T(8,128)(2,1)} %copy-done.4, bf16[16,96,128]{2,1,0:T(8,128)(2,1)} %copy-done, bf16[40,64,640]{2,1,0:T(8,128)(2,1)} %bitcast.11, bf16[40,640,128]{2,1,0:T(8,128)(2,1)} %refs_3_.1, f32[1,32]{1,0:T(1,128)} %bitcast.20), custom_call_target="tpu_custom_call" | custom-call | tf_op jit(solution)/shard_map/legendre_backward/pallas_call | solution.py:434
  110.4 1.8 %all-to-all-done.4.parts = bf16[32,20,128]{2,1,0:T(8,128)(2,1)S(1)} async-done(((bf16[32,20,128]{2,1,0:T(8,128)(2,1)}), bf16[32,20,128]{2,1,0:T(8,128)(2,1)S(1)}, u32[]{:S(2)}, u32[]{:S(2)}) %all-to-all-start.4) | async-done | bytes 163872 | tf_op jit(solution)/shard_map/all_to_all | solution.py:564
  112.3 0.7 weight_gradients.1
Async XLA Ops:
  7.7 25.7 %all-to-all-start = ((bf16[16,160,128]{2,1,0:T(8,128)(2,1)}), bf16[16,160,128]{2,1,0:T(8,128)(2,1)S(1)}, u32[]{:S(2)}, u32[]{:S(2)}) async-start(bf16[16,160,128]{2,1,0:T(8,128)(2,1)} %legendre_forward.3), calls=%async_computation | async-start | bytes 1310720 | tf_op jit(solution)/shard_map/all_to_all | solution.py:544
  33.4 4.4 %copy-start.3 = (bf16[16,160,128]{2,1,0:T(8,128)(2,1)}, bf16[16,160,128]{2,1,0:T(8,128)(2,1)S(1)}, u32[]{:S(2)}) copy-start(bf16[16,160,128]{2,1,0:T(8,128)(2,1)S(1)} %all-to-all-done.refs_0_) | copy-start | bytes 1966084
  33.4 22.4 %all-to-all-start.1 = ((bf16[16,160,128]{2,1,0:T(8,128)(2,1)}), bf16[16,160,128]{2,1,0:T(8,128)(2,1)S(1)}, u32[]{:S(2)}, u32[]{:S(2)}) async-start(bf16[16,160,128]{2,1,0:T(8,128)(2,1)} %legendre_forward.2), calls=%async_computation.1 | async-start | bytes 1310720 | tf_op jit(solution)/shard_map/all_to_all | solution.py:544
  55.9 6.9 %copy-start.2 = (bf16[16,160,128]{2,1,0:T(8,128)(2,1)}, bf16[16,160,128]{2,1,0:T(8,128)(2,1)S(1)}, u32[]{:S(2)}) copy-start(bf16[16,160,128]{2,1,0:T(8,128)(2,1)S(1)} %all-to-all-done.1.refs_0_) | copy-start | bytes 1966084
  55.9 25.1 %all-to-all-start.2 = ((bf16[16,80,128]{2,1,0:T(8,128)(2,1)}), bf16[16,80,128]{2,1,0:T(8,128)(2,1)S(1)}, u32[]{:S(2)}, u32[]{:S(2)}) async-start(bf16[16,80,128]{2,1,0:T(8,128)(2,1)} %get-tuple-element.21), calls=%async_computation.2 | async-start | bytes 655360 | tf_op jit(solution)/shard_map/all_to_all | solution.py:560
  81.0 21.5 %copy-start.4 = (bf16[16,80,128]{2,1,0:T(8,128)(2,1)}, bf16[16,80,128]{2,1,0:T(8,128)(2,1)S(1)}, u32[]{:S(2)}) copy-start(bf16[16,80,128]{2,1,0:T(8,128)(2,1)S(1)} %all-to-all-done.2.refs_0_) | copy-start | bytes 983044
  98.2 4.3 %copy-start = (bf16[16,96,128]{2,1,0:T(8,128)(2,1)}, bf16[16,96,128]{2,1,0:T(8,128)(2,1)S(1)}, u32[]{:S(2)}) copy-start(bf16[16,96,128]{2,1,0:T(8,128)(2,1)S(1)} %all_to_all.25.refs_1_.arrived) | copy-start | bytes 1179652
  98.2 0.7 copy-start.1
  99.6 12.7 %all-to-all-start.4 = ((bf16[32,20,128]{2,1,0:T(8,128)(2,1)}), bf16[32,20,128]{2,1,0:T(8,128)(2,1)S(1)}, u32[]{:S(2)}, u32[]{:S(2)}) async-start(bf16[32,20,128]{2,1,0:T(8,128)(2,1)} %collect_gradients.1), calls=%async_computation.4 | async-start | bytes 393216 | tf_op jit(solution)/shard_map/all_to_all | solution.py:564

commit v3 on v1

--- a/solution.py
+++ b/solution.py
@@ -140,7 +140,7 @@
             pltpu.VMEM(spectral.shape, BF16),
             pltpu.VMEM(cot.shape, BF16),
             pltpu.VMEM(legendre.shape, BF16),
-            pltpu.VMEM((lat // PARTS * own, 2 * width), F32),
+            pltpu.VMEM(((lat // PARTS + 1) * own, 2 * width), F32),
             pltpu.VMEM((width, degrees), F32),
             pltpu.SemaphoreType.DMA((own // block, 3)),
         ],
@@ -445,7 +445,7 @@
             pltpu.VMEM(legendre.shape, BF16),
             pltpu.VMEM(damping.shape, F32),
             pltpu.VMEM(cot.shape, F32),
-            pltpu.VMEM((PARTS * ranks * near * own, 2 * width), F32),
+            pltpu.VMEM(((PARTS * ranks * near + 1) * own, 2 * width), F32),
             pltpu.VMEM((width, degrees), F32),
             pltpu.SemaphoreType.DMA((own // block, 2)),
             pltpu.SemaphoreType.DMA((own // block,)),

time: 113 us -> 113 us (level)
  no operation moved by 1% of the time
where the time goes in v3:
time: 113 us
  Pallas kernels  60.9 us (54%)
  starting transfers between devices  22.5 us (20%)
  blocking collectives  17.2 us (15%)
  waiting for transfers between devices  10.6 us (9%)
    pallas_call x2, Pallas kernels, columns(): pl.pallas_call(functools.partial(column_kernel, ranks, own, not before, l...  35.9 us
    all_to_all x1, blocking collectives, body(): returned.append(exchange(back))  17.2 us
    pallas_call x2, Pallas kernels, forward(): pl.pallas_call(functools.partial(forward_kernel, ranks, block, part), gri...  14.1 us
    all_to_all x2, starting transfers between devices, body(): arrived.append(exchange(sent))  12.7 us
    all_to_all x2, waiting for transfers between devices, body(): arrived.append(exchange(sent))  8.75 us
    pallas_call x1, Pallas kernels, backward(): pl.pallas_call(functools.partial(backward_kernel, ranks, near, block, 2),...  7.94 us
    all_to_all x1, starting transfers between devices, body(): returned.append(exchange(back))  6.92 us
    all_to_all x1, starting transfers between devices, body(): lax.all_to_all(spread, ('grp', 'lat'), split_axis=0, concat_axis=0, tiled...  2.87 us
  transfers between devices with their start and end apart: 4, of which 2 were waited for; matrix products, arithmetic and copies ran while one was open for 0% of the time, Pallas kernels for 47%

profile of v3, /device:TPU:0, one launch (start us, length us, event | category | flops | bytes accessed | tf_op | source)
XLA Modules:
  0.0 112.7 jit_solution(3046838454192457506)
XLA Ops:
  0.6 7.0 %legendre_forward.3 = bf16[16,160,128]{2,1,0:T(8,128)(2,1)} custom-call(bf16[40,64,640]{2,1,0:T(8,128)(2,1)} %bitcast.12, bf16[40,64,640]{2,1,0:T(8,128)(2,1)} %bitcast.9, bf16[40,640,128]{2,1,0:T(8,128)(2,1)} %refs_3_.1, f32[1,32]{1,0:T(1,128)} %bitcast.18, f32[1,128]{1,0:T(1,128)} %bitcast.22), custom_call_target="tpu_custom_call" | custom-call | tf_op jit(solution)/shard_map/legendre_forward/pallas_call | solution.py:133
  7.7 8.3 %all-to-all-start = ((bf16[16,160,128]{2,1,0:T(8,128)(2,1)}), bf16[16,160,128]{2,1,0:T(8,128)(2,1)S(1)}, u32[]{:S(2)}, u32[]{:S(2)}) async-start(bf16[16,160,128]{2,1,0:T(8,128)(2,1)} %legendre_forward.3), calls=%async_computation | async-start | bytes 1310720 | tf_op jit(solution)/shard_map/all_to_all | solution.py:546
  16.0 7.0 %legendre_forward.2 = bf16[16,160,128]{2,1,0:T(8,128)(2,1)} custom-call(bf16[40,64,640]{2,1,0:T(8,128)(2,1)} %bitcast.13, bf16[40,64,640]{2,1,0:T(8,128)(2,1)} %bitcast.10, bf16[40,640,128]{2,1,0:T(8,128)(2,1)} %refs_3_.1, f32[1,32]{1,0:T(1,128)} %bitcast.19, f32[1,128]{1,0:T(1,128)} %bitcast.23), custom_call_target="tpu_custom_call" | custom-call | tf_op jit(solution)/shard_map/legendre_forward/pallas_call | solution.py:133
  23.1 1.6 %column_weights.1.refs_3_ = bf16[1024,80]{1,0:T(8,128)(2,1)} custom-call(bf16[32,512]{1,0:T(8,128)(2,1)} %bitcast.15, f32[1,512]{1,0:T(1,128)} %bitcast.21, bf16[32,512]{1,0:T(8,128)(2,1)} %w_out.1), custom_call_target="tpu_custom_call" | custom-call | tf_op jit(solution)/shard_map/column_weights/pallas_call | solution.py:184
  24.7 8.7 %all-to-all-done.refs_0_ = bf16[16,160,128]{2,1,0:T(8,128)(2,1)S(1)} async-done(((bf16[16,160,128]{2,1,0:T(8,128)(2,1)}), bf16[16,160,128]{2,1,0:T(8,128)(2,1)S(1)}, u32[]{:S(2)}, u32[]{:S(2)}) %all-to-all-start) | async-done | bytes 655392 | tf_op jit(solution)/shard_map/all_to_all | solution.py:546
  33.4 0.0 copy-start.3
  33.4 4.4 %all-to-all-start.1 = ((bf16[16,160,128]{2,1,0:T(8,128)(2,1)}), bf16[16,160,128]{2,1,0:T(8,128)(2,1)S(1)}, u32[]{:S(2)}, u32[]{:S(2)}) async-start(bf16[16,160,128]{2,1,0:T(8,128)(2,1)} %legendre_forward.2), calls=%async_computation.1 | async-start | bytes 1310720 | tf_op jit(solution)/shard_map/all_to_all | solution.py:546
  37.8 0.0 copy-done.3
  37.9 17.9 %column_physics.2 = (bf16[16,80,128]{2,1,0:T(8,128)(2,1)}, f32[1024,80]{1,0:T(8,128)}) custom-call(bf16[16,160,128]{2,1,0:T(8,128)(2,1)} %copy-done.3, bf16[1280,1280]{1,0:T(8,128)(2,1)} %constant.2.clone.refs_1_, bf16[32,512]{1,0:T(8,128)(2,1)} %bitcast.16, bf16[1024,80]{1,0:T(8,128)(2,1)} %column_weights.1.refs_3_), custom_call_target="tpu_custom_call" | custom-call | tf_op jit(solution)/shard_map/column_physics/pallas_call | solution.py:337
  55.7 0.0 all-to-all-done.1.refs_0_
  55.7 0.0 copy-start.2
  55.7 6.9 %all-to-all-start.2 = ((bf16[16,80,128]{2,1,0:T(8,128)(2,1)}), bf16[16,80,128]{2,1,0:T(8,128)(2,1)S(1)}, u32[]{:S(2)}, u32[]{:S(2)}) async-start(bf16[16,80,128]{2,1,0:T(8,128)(2,1)} %get-tuple-element.21), calls=%async_computation.2 | async-start | bytes 655360 | tf_op jit(solution)/shard_map/all_to_all | solution.py:562
  62.7 0.0 copy-done.2
  62.7 18.1 %column_physics.3 = (bf16[16,96,128]{2,1,0:T(8,128)(2,1)}, f32[1,512]{1,0:T(1,128)}) custom-call(bf16[16,160,128]{2,1,0:T(8,128)(2,1)} %copy-done.2, bf16[1280,1280]{1,0:T(8,128)(2,1)} %constant.2.clone.refs_1_, bf16[32,512]{1,0:T(8,128)(2,1)} %bitcast.17, bf16[1024,80]{1,0:T(8,128)(2,1)} %column_weights.1.refs_3_, f32[1024,80]{1,0:T(8,128)} %get-tuple-element.19.refs_4_), custom_call_target="tpu_custom_call" | custom-call | tf_op jit(solution)/shard_map/column_physics/pallas_call | solution.py:337
  80.7 0.0 all-to-all-done.2.refs_0_
  80.8 0.0 copy-start.4
  80.8 17.2 %all_to_all.25.refs_1_.arrived = bf16[16,96,128]{2,1,0:T(8,128)(2,1)S(1)} all-to-all(bf16[16,96,128]{2,1,0:T(8,128)(2,1)} %get-tuple-element.23), channel_id=1, replica_groups=mesh['grp'=2,'lat'=16] {'lat'}, dimensions={0} | all-to-all | bytes 786432 | tf_op jit(solution)/shard_map/all_to_all | solution.py:562
  98.0 0.0 copy-start
  98.0 0.0 copy-start.1
  98.0 0.7 copy-done.1
  98.6 0.7 collect_gradients.1
  99.3 2.9 %all-to-all-start.4 = ((bf16[32,20,128]{2,1,0:T(8,128)(2,1)}), bf16[32,20,128]{2,1,0:T(8,128)(2,1)S(1)}, u32[]{:S(2)}, u32[]{:S(2)}) async-start(bf16[32,20,128]{2,1,0:T(8,128)(2,1)} %collect_gradients.1), calls=%async_computation.4 | async-start | bytes 393216 | tf_op jit(solution)/shard_map/all_to_all | solution.py:566
  102.2 0.0 copy-done.4
  102.2 0.0 copy-done
  102.2 7.9 %legendre_backward.1 = f32[40,64,640]{2,1,0:T(8,128)} custom-call(bf16[16,80,128]{2,1,0:T(8,128)(2,1)} %copy-done.4, bf16[16,96,128]{2,1,0:T(8,128)(2,1)} %copy-done, bf16[40,64,640]{2,1,0:T(8,128)(2,1)} %bitcast.11, bf16[40,640,128]{2,1,0:T(8,128)(2,1)} %refs_3_.1, f32[1,32]{1,0:T(1,128)} %bitcast.20), custom_call_target="tpu_custom_call" | custom-call | tf_op jit(solution)/shard_map/legendre_backward/pallas_call | solution.py:436
  110.2 1.8 %all-to-all-done.4.parts = bf16[32,20,128]{2,1,0:T(8,128)(2,1)S(1)} async-done(((bf16[32,20,128]{2,1,0:T(8,128)(2,1)}), bf16[32,20,128]{2,1,0:T(8,128)(2,1)S(1)}, u32[]{:S(2)}, u32[]{:S(2)}) %all-to-all-start.4) | async-done | bytes 163872 | tf_op jit(solution)/shard_map/all_to_all | solution.py:566
  112.0 0.7 weight_gradients.1
Async XLA Ops:
  7.7 25.7 %all-to-all-start = ((bf16[16,160,128]{2,1,0:T(8,128)(2,1)}), bf16[16,160,128]{2,1,0:T(8,128)(2,1)S(1)}, u32[]{:S(2)}, u32[]{:S(2)}) async-start(bf16[16,160,128]{2,1,0:T(8,128)(2,1)} %legendre_forward.3), calls=%async_computation | async-start | bytes 1310720 | tf_op jit(solution)/shard_map/all_to_all | solution.py:546
  33.4 4.4 %copy-start.3 = (bf16[16,160,128]{2,1,0:T(8,128)(2,1)}, bf16[16,160,128]{2,1,0:T(8,128)(2,1)S(1)}, u32[]{:S(2)}) copy-start(bf16[16,160,128]{2,1,0:T(8,128)(2,1)S(1)} %all-to-all-done.refs_0_) | copy-start | bytes 1966084
  33.4 22.3 %all-to-all-start.1 = ((bf16[16,160,128]{2,1,0:T(8,128)(2,1)}), bf16[16,160,128]{2,1,0:T(8,128)(2,1)S(1)}, u32[]{:S(2)}, u32[]{:S(2)}) async-start(bf16[16,160,128]{2,1,0:T(8,128)(2,1)} %legendre_forward.2), calls=%async_computation.1 | async-start | bytes 1310720 | tf_op jit(solution)/shard_map/all_to_all | solution.py:546
  55.7 6.9 %copy-start.2 = (bf16[16,160,128]{2,1,0:T(8,128)(2,1)}, bf16[16,160,128]{2,1,0:T(8,128)(2,1)S(1)}, u32[]{:S(2)}) copy-start(bf16[16,160,128]{2,1,0:T(8,128)(2,1)S(1)} %all-to-all-done.1.refs_0_) | copy-start | bytes 1966084
  55.7 25.0 %all-to-all-start.2 = ((bf16[16,80,128]{2,1,0:T(8,128)(2,1)}), bf16[16,80,128]{2,1,0:T(8,128)(2,1)S(1)}, u32[]{:S(2)}, u32[]{:S(2)}) async-start(bf16[16,80,128]{2,1,0:T(8,128)(2,1)} %get-tuple-element.21), calls=%async_computation.2 | async-start | bytes 655360 | tf_op jit(solution)/shard_map/all_to_all | solution.py:562
  80.8 21.5 %copy-start.4 = (bf16[16,80,128]{2,1,0:T(8,128)(2,1)}, bf16[16,80,128]{2,1,0:T(8,128)(2,1)S(1)}, u32[]{:S(2)}) copy-start(bf16[16,80,128]{2,1,0:T(8,128)(2,1)S(1)} %all-to-all-done.2.refs_0_) | copy-start | bytes 983044
  98.0 4.3 %copy-start = (bf16[16,96,128]{2,1,0:T(8,128)(2,1)}, bf16[16,96,128]{2,1,0:T(8,128)(2,1)S(1)}, u32[]{:S(2)}) copy-start(bf16[16,96,128]{2,1,0:T(8,128)(2,1)S(1)} %all_to_all.25.refs_1_.arrived) | copy-start | bytes 1179652
  98.0 0.7 copy-start.1
  99.3 12.7 %all-to-all-start.4 = ((bf16[32,20,128]{2,1,0:T(8,128)(2,1)}), bf16[32,20,128]{2,1,0:T(8,128)(2,1)S(1)}, u32[]{:S(2)}, u32[]{:S(2)}) async-start(bf16[32,20,128]{2,1,0:T(8,128)(2,1)} %collect_gradients.1), calls=%async_computation.4 | async-start | bytes 393216 | tf_op jit(solution)/shard_map/all_to_all | solution.py:566
